TPU v7x, 256 devices: a whole 4x4x8 slice. The times are simulated.
256 devices in a mesh: tm: 128 (over y_hi, x, z, core), chan: 2 (over y_lo).
Axes of the slice: x: 4, y: 4 (y_hi: 2, y_lo: 2; y = y_hi * 2 + y_lo), z: 8, core: 2. Of those that a mesh axis runs over, the one named last changes fastest.
Arguments:
- series: float32 [64, 65536], P('chan', 'tm'), may hold values from -200 to 200
- tail: float32 [64, 127], P('chan'), may hold values from -200 to 200
- excl: int32 [1], replicated, may hold values from 32 to 128
Outputs:
- profile: float32 [65536], P('tm')
All inputs are finite; a program needn't handle non-finite values.
Results may differ from a plain program's by a relative error of at most 0.0003.
Values may be sent and summed in bfloat16 or wider, within the bound.
A program may use at most 128 MiB of HBM per device.

v0:
```python
import math

import jax
import jax.numpy as jnp
from jax import lax
from jax.sharding import PartitionSpec as P

C = 64


EPSILON = 1e-05
CEILING = 4.0


def from_behind(shard, axis, by):
    length = lax.axis_size(axis)
    pairs = [(i, i + by) for i in range(length) if 0 <= i + by < length]
    return lax.ppermute(shard, axis, pairs)


def normalize(extended, count, length, channels):
    starts = (
        jnp.arange(length, dtype=jnp.int32)[:, None] + jnp.arange(count, dtype=jnp.int32)[None, :]
    )
    windows = extended[:, starts]
    center = jnp.mean(windows, axis=1, keepdims=True)
    shifted = windows - center
    spread = jnp.mean(shifted * shifted, axis=1, keepdims=True)
    factor = lax.rsqrt(spread + EPSILON) * (1.0 / math.sqrt(length * channels))
    return (shifted * factor).astype(jnp.bfloat16)


def correlate(left, right):
    return lax.dot_general(
        left, right, (((0, 1), (0, 1)), ((), ())), preferred_element_type=jnp.float32
    )


def on_device(series, tail, excl):
    count = series.shape[1]
    width = tail.shape[1]
    length = width + 1
    blocks = lax.axis_size("tm")
    block_index = lax.axis_index("tm")
    head = from_behind(series[:, :width], "tm", -1)
    head = jnp.where(block_index == blocks - 1, tail, head)
    extended = jnp.concatenate([series, head], axis=1)
    query = normalize(extended, count, length, C)
    nearby = from_behind(query, "tm", -1)
    faraway = from_behind(query, "tm", -2)
    limit = excl[0]

    def scored(total, row_pos, offset):
        columns = (block_index + offset) * count + jnp.arange(count, dtype=jnp.int32)[None, :]
        keep = (jnp.abs(row_pos - columns) >= limit) & (block_index + offset < blocks)
        return jnp.where(keep, 1.0 - total, CEILING)

    row_pos = block_index * count + jnp.arange(count, dtype=jnp.int32)[:, None]

    def summed(right, offset):
        total = lax.psum(correlate(query, right), "chan")
        return scored(total, row_pos, offset)

    own_scores = summed(query, 0)
    near_scores = summed(nearby, 1)
    far_scores = summed(faraway, 2)
    row_best = jnp.minimum(
        jnp.min(own_scores, axis=1),
        jnp.minimum(jnp.min(near_scores, axis=1), jnp.min(far_scores, axis=1)),
    )
    near_cols = jnp.min(near_scores, axis=0)
    far_cols = jnp.min(far_scores, axis=0)
    near_home = from_behind(CEILING - near_cols, "tm", 1)
    far_home = from_behind(CEILING - far_cols, "tm", 2)
    return jnp.minimum(row_best, jnp.minimum(CEILING - near_home, CEILING - far_home))


def solution(mesh):
    placed = (P("chan", "tm"), P("chan", None), P())
    return jax.shard_map(on_device, mesh=mesh, in_specs=placed, out_specs=P("tm"), check_vma=False)
```

profile of v0, /device:TPU:199, one launch (start us, length us, event | category | flops | bytes accessed | tf_op | source)
XLA Modules:
  0.0 527.9 jit_solution(6740007756492926485)
XLA Ops:
  6.5 0.7 slice.3
  7.3 2.6 collective-permute-start
  10.0 2.3 collective-permute-done
  12.3 0.8 pad_maximum_fusion
  13.2 0.2 copy.18
  13.3 215.5 %gather_fusion = f32[65536,32]{1,0:T(8,128)} fusion(f32[32,639]{0,1:T(8,128)S(1)} %copy.18, s32[65536]{0:T(1024)S(1)} %broadcast_clamp_fusion), kind=kCustom, calls=%fused_computation | custom fusion | bytes 17039360 | tf_op jit(solution)/shard_map/gather | solution.py:25
  228.8 22.1 %copy.26 = f32[128,512,32]{1,0,2:T(8,128)} copy(f32[128,512,32]{2,1,0:T(8,128)} %bitcast.26) | data formatting | bytes 16777216 | tf_op jit(solution)/shard_map/gather | solution.py:25
  250.9 4.7 bitcast_reduce_fusion
  255.7 1.0 copy-done
  256.7 1.4 multiply_reduce_fusion
  258.2 1.7 multiply_convert_fusion
  259.9 1.9 collective-permute-start.1
  261.8 2.8 collective-permute-start.2
  264.6 3.4 convolution_bitcast_fusion.2
  268.0 80.2 %collective-permute-done.1 = bf16[32,128,512]{2,1,0:T(8,128)(2,1)S(1)} collective-permute-done((bf16[32,128,512]{2,1,0:T(8,128)(2,1)S(1)}, bf16[32,128,512]{2,1,0:T(8,128)(2,1)S(1)}, u32[]{:S(2)}, u32[]{:S(2)}) %collective-permute-start.1) | collective-permute-done | bytes 4194336 | tf_op jit(solution)/shard_map/ppermute | solution.py:18
  348.2 3.4 convolution_bitcast_fusion.1
  351.6 9.8 %collective-permute-done.2 = bf16[32,128,512]{2,1,0:T(8,128)(2,1)S(1)} collective-permute-done((bf16[32,128,512]{2,1,0:T(8,128)(2,1)S(1)}, bf16[32,128,512]{2,1,0:T(8,128)(2,1)S(1)}, u32[]{:S(2)}, u32[]{:S(2)}) %collective-permute-start.2) | collective-permute-done | bytes 4194336 | tf_op jit(solution)/shard_map/ppermute | solution.py:18
  361.4 3.4 convolution_bitcast_fusion
  365.4 144.6 %all-reduce.3.cloned.1.call-done = (f32[512,512]{1,0:T(8,128)}, f32[512,512]{1,0:T(8,128)}, f32[512,512]{1,0:T(8,128)}) async-done(((f32[512,512]{1,0:T(8,128)}, f32[512,512]{1,0:T(8,128)}, f32[512,512]{1,0:T(8,128)}), (f32[512,512]{1,0:T(8,128)}, f32[512,512]{1,0:T(8,128)}, f32[512,512]{1,0:T(8,128)})) %all-reduce.3.cloned.1.call-update) | async-done | bytes 3145744 | tf_op jit(solution)/shard_map/psum | solution.py:61
  510.0 3.2 fusion.6
  513.2 2.8 collective-permute-start.3
  516.0 3.7 collective-permute-start.4
  519.7 0.7 collective-permute-done.4
  520.5 0.6 minimum_minimum_fusion
  (14 shorter events, 0.2 us)
Async XLA Ops:
  6.5 503.4 %all-reduce.3.cloned.1.call-start = ((), (), s32[]{:S(2)}) async-start(), calls=%async_computation | async-start | bytes 6291456 | tf_op jit(solution)/shard_map/psum | solution.py:61
  7.3 5.0 collective-permute-start
  250.9 5.8 %copy-start = (f32[128,512,32]{1,0,2:T(8,128)S(1)}, f32[128,512,32]{1,0,2:T(8,128)}, u32[]{:S(2)}) copy-start(f32[128,512,32]{1,0,2:T(8,128)} %copy.26) | copy-start | bytes 25165828
  259.9 88.3 %collective-permute-start.1 = (bf16[32,128,512]{2,1,0:T(8,128)(2,1)S(1)}, bf16[32,128,512]{2,1,0:T(8,128)(2,1)S(1)}, u32[]{:S(2)}, u32[]{:S(2)}) collective-permute-start(bf16[32,128,512]{2,1,0:T(8,128)(2,1)S(1)} %multiply_convert_fusion), channel_id=1, source_target_pairs={{2,0},{4,2},{6,4},{8,6},{10,8},{12,10},{14,12},{16,14},{18,16},{20... | collective-permute-start | bytes 12582920 | tf_op jit(solution)/shard_map/ppermute | solution.py:18
  261.8 99.6 %collective-permute-start.2 = (bf16[32,128,512]{2,1,0:T(8,128)(2,1)S(1)}, bf16[32,128,512]{2,1,0:T(8,128)(2,1)S(1)}, u32[]{:S(2)}, u32[]{:S(2)}) collective-permute-start(bf16[32,128,512]{2,1,0:T(8,128)(2,1)S(1)} %multiply_convert_fusion), channel_id=1, source_target_pairs={{4,0},{6,2},{8,4},{10,6},{12,8},{14,10},{16,12},{18,14},{20,16},{2... | collective-permute-start | bytes 12582920 | tf_op jit(solution)/shard_map/ppermute | solution.py:18
  513.2 6.6 %collective-permute-start.3 = (f32[512]{0:T(512)S(1)}, f32[512]{0:T(512)S(1)}, u32[]{:S(2)}, u32[]{:S(2)}) collective-permute-start(f32[512]{0:T(512)S(1)} %broadcast_subtract_fusion.1), channel_id=1, source_target_pairs={{0,2},{2,4},{4,6},{6,8},{8,10},{10,12},{12,14},{14,16},{16,18},{18... | collective-permute-start | bytes 6152 | tf_op jit(solution)/shard_map/ppermute | solution.py:18
  516.0 4.4 collective-permute-start.4
Sparse Core Ops, SparseCore 0:
  364.9 145.0 all-reduce.2
where the time goes:
time: 537 us; the launch traced here: 528 us
  local copies, waits for them, and re-layouts  240 us (45%)
  waiting for transfers between devices  238 us (44%)
  between operations  14.2 us (3%)
  starting transfers between devices  13.8 us (3%)
  other arithmetic  12.6 us (2%)
  matrix products  10.1 us (2%)
    gather x2, local copies, waits for them, and re-layouts, normalize(): windows = extended[:, starts]  238 us
    psum x1, waiting for transfers between devices, summed(): total = lax.psum(correlate(query, right), 'chan')  145 us
    ppermute x5, waiting for transfers between devices, from_behind(): return lax.ppermute(shard, axis, pairs)  93 us
    ppermute x5, starting transfers between devices, from_behind(): return lax.ppermute(shard, axis, pairs)  13.8 us
  transfers between devices with their start and end apart: 6, of which 5 were waited for; matrix products, arithmetic and copies ran while one was open for 1% of the time, Pallas kernels for 0%

commit v1 on v0

v1 whole, which is shorter than its diff:
```python
import math

import jax
import jax.numpy as jnp
from jax import lax
from jax.experimental import pallas as pl
from jax.experimental.pallas import tpu as pltpu
from jax.sharding import PartitionSpec as P

C = 64
M = 128
EPSILON = 1e-05
MASKED = -3.0

BLOCK = 512
HALO = 128
SPAN = BLOCK + HALO
GROUP = 32
COPIES = 4
ROWS = BLOCK + GROUP
MESH = pl.DeviceIdType.MESH
NT = (((1,), (1,)), ((), ()))


def spread_lanes(x):
    parts = [x[:, :ROWS]]
    for a in range(1, COPIES):
        parts.append(pltpu.roll(x, SPAN - GROUP * a, 1)[:, :ROWS])
    return jnp.concatenate(parts, axis=0).T


def statistics(y):
    total, moment, width = y, None, 1
    while width < GROUP:
        left, right = total[:-width], total[width:]
        delta = left - right
        delta = delta * delta * (0.5 / width)
        moment = delta if moment is None else moment[:-width] + moment[width:] + delta
        total = left + right
        width *= 2
    total, moment = total[:BLOCK], moment[:BLOCK]
    while width < M:
        other = pltpu.roll(total, width, 1)
        delta = total - other
        moment = moment + pltpu.roll(moment, width, 1) + delta * delta * (0.5 / width)
        total = total + other
        width *= 2
    center = total * (1.0 / M)
    factor = lax.rsqrt(moment * (1.0 / M) + EPSILON) * (1.0 / math.sqrt(M * C))
    return center, factor


def dot(left, right):
    return lax.dot_general(left, right, NT, preferred_element_type=jnp.float32)


def kernel(
    blocks, series, tail, excl, out,
    own, ahead, head, lanes, center, factor, zed,
    row_out, row_in, col_out, near_in, far_in,
    send, recv,
):
    t = lax.axis_index("tm")
    h = lax.axis_index("chan")

    def at(offset):
        return lax.rem(t + (offset + blocks), blocks)

    barrier = pltpu.get_barrier_semaphore()
    pl.semaphore_signal(barrier, inc=1, device_id=(t, 1 - h), device_id_type=MESH)
    for offset in (1, 2, 3):
        for chan in (0, 1):
            pl.semaphore_signal(
                barrier, inc=1, device_id=(at(offset), chan), device_id_type=MESH
            )
    own[0, :, :BLOCK] = series[...]
    head[...] = jnp.where(
        t == 0, jnp.concatenate([tail[...], jnp.zeros((GROUP, 1), jnp.float32)], axis=1),
        series[:, :HALO],
    )
    pl.semaphore_wait(barrier, 7)

    copies = []

    def push(source, target, index, device):
        copies.append(
            pltpu.make_async_remote_copy(
                src_ref=source,
                dst_ref=target,
                send_sem=send.at[len(copies)],
                recv_sem=recv.at[index],
                device_id=device,
                device_id_type=MESH,
            )
        )
        copies[-1].start()

    slot = (h, 1 - h)
    for chan in (0, 1):
        push(head, own.at[slot[chan], :, BLOCK:], 1 + slot[chan], (at(-1), chan))
    push(series, own.at[1, :, :BLOCK], 0, (t, 1 - h))
    for chan in (0, 1):
        push(series, ahead.at[slot[chan], :, :BLOCK], 3 + slot[chan], (at(-1 - chan), chan))
    for chan in (0, 1):
        push(head, ahead.at[slot[chan], :, BLOCK:], 5 + slot[chan], (at(-2 - chan), chan))

    def arrive(target, index):
        pltpu.make_async_remote_copy(
            src_ref=target,
            dst_ref=target,
            send_sem=send.at[0],
            recv_sem=recv.at[index],
            device_id=(t, 1 - h),
            device_id_type=MESH,
        ).wait_recv()

    def prepare(x, index):
        y = spread_lanes(x)
        lanes[index] = y
        mean, scale = statistics(y)
        center[index] = mean
        factor[index] = scale

    def normalized(index, step):
        parts = []
        for i in (2 * step, 2 * step + 1):
            shifted = lanes[index, i : i + BLOCK, :] - center[index]
            parts.append((shifted * factor[index]).astype(jnp.bfloat16))
        return parts

    half = BLOCK // 2
    same = None
    for s in (0, 1):
        if s == 1:
            arrive(own.at[1, :, :BLOCK], 0)
        arrive(own.at[s, :, BLOCK:], 1 + s)
        prepare(own[s], s)
        for step in range(GROUP // 2):
            parts = normalized(s, step)
            for j in (0, 1):
                zed[GROUP * s + 2 * step + j] = parts[j]
            query = jnp.concatenate(parts, axis=1)
            chosen = jnp.where(h == 0, query[:half], query[half:])
            product = dot(query, chosen)
            same = product if same is None else same + product

    cross = None
    for s in (0, 1):
        arrive(ahead.at[s, :, :BLOCK], 3 + s)
        arrive(ahead.at[s, :, BLOCK:], 5 + s)
        prepare(ahead[s], 2 + s)
        for step in range(GROUP // 2):
            k = GROUP * s + 2 * step
            query = jnp.concatenate([zed[k], zed[k + 1]], axis=1)
            product = dot(query, jnp.concatenate(normalized(2 + s, step), axis=1))
            cross = product if cross is None else cross + product

    limit = excl[0]
    apart = (
        lax.broadcasted_iota(jnp.int32, (BLOCK, half), 0)
        - lax.broadcasted_iota(jnp.int32, (BLOCK, half), 1)
        - half * h
    )
    same = jnp.where(jnp.abs(apart) >= limit, same, MASKED)

    reach = (
        lax.broadcasted_iota(jnp.int32, (HALO, HALO), 1)
        - lax.broadcasted_iota(jnp.int32, (HALO, HALO), 0)
        + (BLOCK * (1 + h) - (BLOCK - HALO))
    )
    corner = jnp.where(reach >= limit, cross[BLOCK - HALO :, :HALO], MASKED)
    first = jnp.concatenate([cross[: BLOCK - HALO, :HALO], corner], axis=0)
    tiles = [first] + [cross[:, HALO * j : HALO * (j + 1)] for j in range(1, BLOCK // HALO)]

    inside = t + 1 + h < blocks
    columns = jnp.concatenate([jnp.max(tile, axis=0, keepdims=True) for tile in tiles], axis=1)
    col_out[...] = jnp.where(inside, columns, MASKED)

    best = tiles[0]
    for tile in tiles[1:]:
        best = jnp.maximum(best, tile)
    best = jnp.where(inside, best, MASKED)
    best = jnp.maximum(best, jnp.maximum(same[:, :HALO], same[:, HALO:]))
    rows = jnp.max(best.T, axis=0, keepdims=True)
    row_out[...] = rows

    @pl.when(h == 0)
    def _():
        for chan in (0, 1):
            near = pltpu.make_async_remote_copy(
                src_ref=col_out, dst_ref=near_in, send_sem=send.at[7 + chan], recv_sem=recv.at[7],
                device_id=(at(1), chan), device_id_type=MESH,
            )
            near.start()

    @pl.when(h == 1)
    def _():
        for chan in (0, 1):
            far = pltpu.make_async_remote_copy(
                src_ref=col_out, dst_ref=far_in, send_sem=send.at[7 + chan], recv_sem=recv.at[8],
                device_id=(at(2), chan), device_id_type=MESH,
            )
            far.start()

    mine = pltpu.make_async_remote_copy(
        src_ref=row_out, dst_ref=row_in, send_sem=send.at[9], recv_sem=recv.at[9],
        device_id=(t, 1 - h), device_id_type=MESH,
    )
    mine.start()
    for copy in copies:
        copy.wait_send()
    arrive(near_in, 7)
    arrive(far_in, 8)
    mine.wait()
    for chan in (0, 1):
        pltpu.make_async_remote_copy(
            src_ref=col_out, dst_ref=near_in, send_sem=send.at[7 + chan], recv_sem=recv.at[7],
            device_id=(t, 1 - h), device_id_type=MESH,
        ).wait_send()
    best = jnp.maximum(jnp.maximum(row_out[...], row_in[...]), jnp.maximum(near_in[...], far_in[...]))
    out[...] = 1.0 - best


def solution(mesh):
    blocks = mesh.shape["tm"]

    def on_device(series, tail, excl):
        vmem = pl.BlockSpec(memory_space=pltpu.VMEM)
        f32 = jnp.float32
        result = pl.pallas_call(
            lambda *refs: kernel(blocks, *refs),
            out_shape=jax.ShapeDtypeStruct((1, BLOCK), f32),
            in_specs=[vmem, vmem, pl.BlockSpec(memory_space=pltpu.SMEM)],
            out_specs=vmem,
            scratch_shapes=[
                pltpu.VMEM((2, GROUP, SPAN), f32),
                pltpu.VMEM((2, GROUP, SPAN), f32),
                pltpu.VMEM((GROUP, HALO), f32),
                pltpu.VMEM((4, ROWS, M), f32),
                pltpu.VMEM((4, BLOCK, M), f32),
                pltpu.VMEM((4, BLOCK, M), f32),
                pltpu.VMEM((2 * GROUP, BLOCK, M), jnp.bfloat16),
            ]
            + [pltpu.VMEM((1, BLOCK), f32)] * 5
            + [pltpu.SemaphoreType.DMA((10,)), pltpu.SemaphoreType.DMA((10,))],
            compiler_params=pltpu.CompilerParams(
                collective_id=0, has_side_effects=True, vmem_limit_bytes=48 * 1024 * 1024
            ),
        )(series, tail, excl)
        return result.reshape(BLOCK)

    placed = (P("chan", "tm"), P("chan", None), P())
    return jax.shard_map(
        on_device, mesh=mesh, in_specs=placed, out_specs=P("tm"), check_vma=False
    )
```

time: 537 us -> 41 us (0.08)
  the two profiles are of different devices: /device:TPU:199 before, /device:TPU:1 now
where the time goes in v1:
time: 41 us; the launch traced here: 40.8 us
  Pallas kernels  38 us (93%)
  local copies, waits for them, and re-layouts  2.13 us (5%)
  between operations  0.67 us (2%)
    pallas_call x1, Pallas kernels, on_device(): pl.pallas_call(lambda *refs: kernel(blocks, *refs), out_shape=jax.ShapeDt...  38 us
    unnamed x5, local copies, waits for them, and re-layouts  2.13 us

profile of v1, /device:TPU:1, one launch (start us, length us, event | category | flops | bytes accessed | tf_op | source)
XLA Modules:
  0.0 40.8 jit_solution(16242560762413299364)
XLA Ops:
  0.7 0.0 copy-start
  0.7 0.8 %copy-done = f32[32,512]{1,0:T(8,128)S(1)} copy-done((f32[32,512]{1,0:T(8,128)S(1)}, f32[32,512]{1,0:T(8,128)}, u32[]{:S(2)}) %copy-start) | copy-done | bytes 65560
  1.5 0.0 copy-start.1
  1.5 0.7 %copy-done.1 = f32[32,127]{1,0:T(8,128)S(1)} copy-done((f32[32,127]{1,0:T(8,128)S(1)}, f32[32,127]{1,0:T(8,128)}, u32[]{:S(2)}) %copy-start.1) | copy-done | bytes 16280
  2.2 38.0 %shard_map.37 = f32[1,512]{1,0:T(1,128)S(1)} custom-call(f32[32,512]{1,0:T(8,128)S(1)} %copy-done, f32[32,127]{1,0:T(8,128)S(1)} %copy-done.1, s32[1]{0:T(128)S(6)} %copy.5.refs_2_), custom_call_target="tpu_custom_call" | custom-call | tf_op jit(solution)/shard_map/pallas_call | solution.py:230
  40.2 0.6 %copy.6 = f32[512]{0:T(512)} copy(f32[512]{0:T(512)S(1)} %bitcast.1) | data formatting | bytes 4096
Async XLA Ops:
  0.7 0.8 %copy-start = (f32[32,512]{1,0:T(8,128)S(1)}, f32[32,512]{1,0:T(8,128)}, u32[]{:S(2)}) copy-start(f32[32,512]{1,0:T(8,128)} %refs_0_.1) | copy-start | bytes 196612
  1.5 0.7 %copy-start.1 = (f32[32,127]{1,0:T(8,128)S(1)}, f32[32,127]{1,0:T(8,128)}, u32[]{:S(2)}) copy-start(f32[32,127]{1,0:T(8,128)} %refs_1_.1) | copy-start | bytes 48772

commit v2 on v1

v2 whole, which is shorter than its diff:
```python
import math

import jax
import jax.numpy as jnp
from jax import lax
from jax.experimental import pallas as pl
from jax.experimental.pallas import tpu as pltpu
from jax.sharding import PartitionSpec as P

C = 64
M = 128
EPSILON = 1e-05
MASKED = -3.0

BLOCK = 512
HALO = 128
SPAN = BLOCK + HALO
GROUP = 32
COPIES = 4
ROWS = BLOCK + GROUP
MESH = pl.DeviceIdType.MESH
NT = (((1,), (1,)), ((), ()))


def spread_lanes(x):
    parts = [x[:, :ROWS]]
    for a in range(1, COPIES):
        parts.append(pltpu.roll(x, SPAN - GROUP * a, 1)[:, :ROWS])
    return jnp.concatenate(parts, axis=0).T


def statistics(y):
    total, moment, width = y, None, 1
    while width < GROUP:
        left, right = total[:-width], total[width:]
        delta = left - right
        delta = delta * delta * (0.5 / width)
        moment = delta if moment is None else moment[:-width] + moment[width:] + delta
        total = left + right
        width *= 2
    total, moment = total[:BLOCK], moment[:BLOCK]
    while width < M:
        other = pltpu.roll(total, width, 1)
        delta = total - other
        moment = moment + pltpu.roll(moment, width, 1) + delta * delta * (0.5 / width)
        total = total + other
        width *= 2
    center = total * (1.0 / M)
    factor = lax.rsqrt(moment * (1.0 / M) + EPSILON) * (1.0 / math.sqrt(M * C))
    return center, factor


def dot(left, right):
    return lax.dot_general(left, right, NT, preferred_element_type=jnp.float32)


def kernel(
    blocks, series, tail, excl, out,
    own, behind, rest, ending, lanes, center, factor, zed,
    row_out, row_in, col_out, near_in, far_in,
    local, send, recv, ready,
):
    t = lax.axis_index("tm")
    h = lax.axis_index("chan")
    after = jnp.minimum(blocks - 1 - t, 2)
    last = t == blocks - 1
    inside = t >= 1 + h

    fetch = pltpu.make_async_copy(series, own.at[0, :, :BLOCK], local.at[0])
    fetch.start()
    barrier = pltpu.get_barrier_semaphore()

    def signal(semaphore, device):
        pl.semaphore_signal(semaphore, inc=1, device_id=device, device_id_type=MESH)

    signal(barrier, (t, 1 - h))

    @pl.when(t >= 1)
    def _():
        for chan in (0, 1):
            signal(barrier, (t - 1, chan))

    @pl.when((h == 1) & (t >= 2))
    def _():
        for chan in (0, 1):
            signal(barrier, (t - 2, chan))

    pl.semaphore_wait(barrier, 1 + after + jnp.minimum(after, 1))

    def push(source, target, outgoing, incoming, device):
        return pltpu.make_async_remote_copy(
            src_ref=source,
            dst_ref=target,
            send_sem=send.at[outgoing],
            recv_sem=recv.at[incoming],
            device_id=device,
            device_id_type=MESH,
        )

    def arrive(target, index):
        push(target, target, 0, index, (t, 1 - h)).wait_recv()

    slot = (h, 1 - h)
    opening = series.at[:, :HALO]
    share = push(series, own.at[1, :, :BLOCK], 0, 0, (t, 1 - h))
    next_block = push(series, behind.at[slot[0], :, :BLOCK], 1, 3 + slot[0], (t + 1, 0))
    next_edge = push(opening, behind.at[slot[1], :, BLOCK:], 2, 5 + slot[1], (t + 1, 1))
    second_block = push(series, behind.at[slot[1], :, :BLOCK], 3, 3 + slot[1], (t + 2, 1))
    edges = [
        push(opening, own.at[slot[c], :, BLOCK:], 4 + c, 1 + slot[c], (t - 1, c)) for c in (0, 1)
    ]
    closing = push(ending, own.at[1, :, BLOCK:], 9, 2, (t, 1 - h))

    @pl.when(after >= 1)
    def _():
        for chan in (0, 1):
            signal(ready, (t + 1, chan))

    share.start()

    @pl.when(after >= 1)
    def _():
        next_block.start()

    @pl.when((after >= 1) & (t >= 1))
    def _():
        next_edge.start()

    @pl.when(after >= 2)
    def _():
        second_block.start()

    @pl.when(t >= 1)
    def _():
        pl.semaphore_wait(ready, 2)
        for edge in edges:
            edge.start()

    fetch.wait()

    @pl.when(last)
    def _():
        copy = pltpu.make_async_copy(tail, rest, local.at[1])
        copy.start()
        copy.wait()
        ending[...] = jnp.concatenate([rest[...], jnp.zeros((GROUP, 1), jnp.float32)], axis=1)
        own[0, :, BLOCK:] = ending[...]
        closing.start()

    @pl.when(jnp.logical_not(inside))
    def _():
        behind[...] = jnp.zeros_like(behind)

    def prepare(x, index):
        y = spread_lanes(x)
        lanes[index] = y
        mean, scale = statistics(y)
        center[index] = mean
        factor[index] = scale

    def normalized(index, step):
        parts = []
        for i in (2 * step, 2 * step + 1):
            shifted = lanes[index, i : i + BLOCK, :] - center[index]
            parts.append((shifted * factor[index]).astype(jnp.bfloat16))
        return parts

    half = BLOCK // 2
    same = None
    for s in (0, 1):
        if s == 1:
            arrive(own.at[1, :, :BLOCK], 0)
            arrive(own.at[1, :, BLOCK:], 2)
        else:

            @pl.when(jnp.logical_not(last))
            def _():
                arrive(own.at[0, :, BLOCK:], 1)

        prepare(own[s], s)
        for step in range(GROUP // 2):
            parts = normalized(s, step)
            for j in (0, 1):
                zed[GROUP * s + 2 * step + j] = parts[j]
            query = jnp.concatenate(parts, axis=1)
            chosen = jnp.where(h == 0, query[:half], query[half:])
            product = dot(query, chosen)
            same = product if same is None else same + product

    cross = None
    for s in (0, 1):

        @pl.when(inside)
        def _(s=s):
            arrive(behind.at[s, :, :BLOCK], 3 + s)

        @pl.when(inside & (h == 1))
        def _(s=s):
            arrive(behind.at[s, :, BLOCK:], 5 + s)

        edge = jnp.where(h == 0, own[s, :, :HALO], behind[s, :, BLOCK:])
        prepare(jnp.concatenate([behind[s, :, :BLOCK], edge], axis=1), 2 + s)
        for step in range(GROUP // 2):
            k = GROUP * s + 2 * step
            query = jnp.concatenate([zed[k], zed[k + 1]], axis=1)
            product = dot(query, jnp.concatenate(normalized(2 + s, step), axis=1))
            cross = product if cross is None else cross + product

    limit = excl[0]
    apart = (
        lax.broadcasted_iota(jnp.int32, (BLOCK, half), 0)
        - lax.broadcasted_iota(jnp.int32, (BLOCK, half), 1)
        - half * h
    )
    same = jnp.where(jnp.abs(apart) >= limit, same, MASKED)

    reach = (
        lax.broadcasted_iota(jnp.int32, (HALO, HALO), 0)
        - lax.broadcasted_iota(jnp.int32, (HALO, HALO), 1)
        + (HALO + BLOCK * h)
    )
    corner = jnp.where(reach >= limit, cross[:HALO, BLOCK - HALO :], MASKED)
    final = jnp.concatenate([corner, cross[HALO:, BLOCK - HALO :]], axis=0)
    tiles = [cross[:, HALO * j : HALO * (j + 1)] for j in range(BLOCK // HALO - 1)] + [final]

    columns = jnp.concatenate([jnp.max(tile, axis=0, keepdims=True) for tile in tiles], axis=1)
    col_out[...] = columns

    home = [push(col_out, near_in, 6 + c, 7, (t - 1, c)) for c in (0, 1)]
    home_far = [push(col_out, far_in, 6 + c, 8, (t - 2, c)) for c in (0, 1)]

    @pl.when(inside & (h == 0))
    def _():
        for copy in home:
            copy.start()

    @pl.when(inside & (h == 1))
    def _():
        for copy in home_far:
            copy.start()

    best = tiles[0]
    for tile in tiles[1:]:
        best = jnp.maximum(best, tile)
    best = jnp.where(inside, best, MASKED)
    best = jnp.maximum(best, jnp.maximum(same[:, :HALO], same[:, HALO:]))
    rows = jnp.max(best.T, axis=0, keepdims=True)
    row_out[...] = rows

    mine = push(row_out, row_in, 8, 9, (t, 1 - h))
    mine.start()
    share.wait_send()

    @pl.when(after >= 1)
    def _():
        next_block.wait_send()
        arrive(near_in, 7)

    @pl.when((after >= 1) & (t >= 1))
    def _():
        next_edge.wait_send()

    @pl.when(after >= 2)
    def _():
        second_block.wait_send()
        arrive(far_in, 8)

    @pl.when(after < 1)
    def _():
        near_in[...] = jnp.full_like(near_in, MASKED)
        closing.wait_send()

    @pl.when(after < 2)
    def _():
        far_in[...] = jnp.full_like(far_in, MASKED)

    @pl.when(t >= 1)
    def _():
        for edge in edges:
            edge.wait_send()

    @pl.when(inside)
    def _():
        for copy in home:
            copy.wait_send()

    mine.wait()
    best = jnp.maximum(jnp.maximum(row_out[...], row_in[...]), jnp.maximum(near_in[...], far_in[...]))
    out[...] = 1.0 - best


def solution(mesh):
    blocks = mesh.shape["tm"]

    def on_device(series, tail, excl):
        vmem = pl.BlockSpec(memory_space=pltpu.VMEM)
        hbm = pl.BlockSpec(memory_space=pl.ANY)
        f32 = jnp.float32
        result = pl.pallas_call(
            lambda *refs: kernel(blocks, *refs),
            out_shape=jax.ShapeDtypeStruct((1, BLOCK), f32),
            in_specs=[hbm, hbm, pl.BlockSpec(memory_space=pltpu.SMEM)],
            out_specs=vmem,
            scratch_shapes=[
                pltpu.VMEM((2, GROUP, SPAN), f32),
                pltpu.VMEM((2, GROUP, SPAN), f32),
                pltpu.VMEM((GROUP, M - 1), f32),
                pltpu.VMEM((GROUP, HALO), f32),
                pltpu.VMEM((4, ROWS, M), f32),
                pltpu.VMEM((4, BLOCK, M), f32),
                pltpu.VMEM((4, BLOCK, M), f32),
                pltpu.VMEM((2 * GROUP, BLOCK, M), jnp.bfloat16),
            ]
            + [pltpu.VMEM((1, BLOCK), f32)] * 5
            + [
                pltpu.SemaphoreType.DMA((2,)),
                pltpu.SemaphoreType.DMA((10,)),
                pltpu.SemaphoreType.DMA((10,)),
                pltpu.SemaphoreType.REGULAR,
            ],
            compiler_params=pltpu.CompilerParams(
                collective_id=0, has_side_effects=True, vmem_limit_bytes=64 * 1024 * 1024
            ),
        )(series, tail, excl)
        return result.reshape(BLOCK)

    placed = (P("chan", "tm"), P("chan", None), P())
    return jax.shard_map(
        on_device, mesh=mesh, in_specs=placed, out_specs=P("tm"), check_vma=False
    )
```

time: 41 us -> 30.2 us (0.74)
  the two profiles are of different devices: /device:TPU:1 before, /device:TPU:199 now
where the time goes in v2:
time: 30.2 us; the launch traced here: 29.6 us
  Pallas kernels  27.7 us (92%)
  local copies, waits for them, and re-layouts  1.26 us (4%)
  between operations  0.66 us (2%)
    pallas_call x1, Pallas kernels, on_device(): pl.pallas_call(lambda *refs: kernel(blocks, *refs), out_shape=jax.ShapeDt...  27.7 us
    unnamed x1, local copies, waits for them, and re-layouts  1.26 us

profile of v2, /device:TPU:199, one launch (start us, length us, event | category | flops | bytes accessed | tf_op | source)
XLA Modules:
  0.0 29.6 jit_solution(2082314984718213875)
XLA Ops:
  0.7 27.7 %shard_map.37 = f32[1,512]{1,0:T(1,128)} custom-call(f32[32,512]{1,0:T(8,128)} %refs_0_.1, f32[32,127]{1,0:T(8,128)} %refs_1_.1, s32[1]{0:T(128)S(6)} %copy.5.refs_2_), custom_call_target="tpu_custom_call" | custom-call | tf_op jit(solution)/shard_map/pallas_call | solution.py:299
  28.3 1.3 %copy.6 = f32[512]{0:T(512)} copy(f32[512]{0:T(512)} %bitcast.1) | data formatting | bytes 4096

commit v3 on v2

--- a/solution.py
+++ b/solution.py
@@ -18,6 +18,7 @@
 GROUP = 32
 COPIES = 4
 ROWS = BLOCK + GROUP
+ROW = 16
 MESH = pl.DeviceIdType.MESH
 NT = (((1,), (1,)), ((), ()))
 
@@ -54,6 +55,12 @@
     return lax.dot_general(left, right, NT, preferred_element_type=jnp.float32)
 
 
+def accumulate(totals, products):
+    if totals is None:
+        return products
+    return [total + product for total, product in zip(totals, products)]
+
+
 def kernel(
     blocks, series, tail, excl, out,
     own, behind, rest, ending, lanes, center, factor, zed,
@@ -73,7 +80,14 @@
     def signal(semaphore, device):
         pl.semaphore_signal(semaphore, inc=1, device_id=device, device_id_type=MESH)
 
+    opens_row = lax.rem(t, ROW) == 0
+    closes_row = lax.rem(t, ROW) == ROW - 1
     signal(barrier, (t, 1 - h))
+
+    @pl.when((after >= 1) & jnp.logical_not(closes_row))
+    def _():
+        for chan in (0, 1):
+            signal(barrier, (t + 1, chan))
 
     @pl.when(t >= 1)
     def _():
@@ -85,7 +99,7 @@
         for chan in (0, 1):
             signal(barrier, (t - 2, chan))
 
-    pl.semaphore_wait(barrier, 1 + after + jnp.minimum(after, 1))
+    pl.semaphore_wait(barrier, 1 + after + jnp.minimum(after, 1) + 2 * jnp.minimum(lax.rem(t, ROW), 1))
 
     def push(source, target, outgoing, incoming, device):
         return pltpu.make_async_remote_copy(
@@ -111,11 +125,16 @@
     ]
     closing = push(ending, own.at[1, :, BLOCK:], 9, 2, (t, 1 - h))
 
-    @pl.when(after >= 1)
+    @pl.when((after >= 1) & closes_row)
     def _():
         for chan in (0, 1):
             signal(ready, (t + 1, chan))
 
+    @pl.when(jnp.logical_not(opens_row))
+    def _():
+        for edge in edges:
+            edge.start()
+
     share.start()
 
     @pl.when(after >= 1)
@@ -130,7 +149,7 @@
     def _():
         second_block.start()
 
-    @pl.when(t >= 1)
+    @pl.when(opens_row & (t >= 1))
     def _():
         pl.semaphore_wait(ready, 2)
         for edge in edges:
@@ -167,16 +186,14 @@
 
     half = BLOCK // 2
     same = None
+
+    @pl.when(jnp.logical_not(last))
+    def _():
+        arrive(own.at[0, :, BLOCK:], 1)
+
+    arrive(own.at[1, :, BLOCK:], 2)
+    arrive(own.at[1, :, :BLOCK], 0)
     for s in (0, 1):
-        if s == 1:
-            arrive(own.at[1, :, :BLOCK], 0)
-            arrive(own.at[1, :, BLOCK:], 2)
-        else:
-
-            @pl.when(jnp.logical_not(last))
-            def _():
-                arrive(own.at[0, :, BLOCK:], 1)
-
         prepare(own[s], s)
         for step in range(GROUP // 2):
             parts = normalized(s, step)
@@ -184,28 +201,30 @@
                 zed[GROUP * s + 2 * step + j] = parts[j]
             query = jnp.concatenate(parts, axis=1)
             chosen = jnp.where(h == 0, query[:half], query[half:])
-            product = dot(query, chosen)
-            same = product if same is None else same + product
+            same = accumulate(same, [dot(query[:half], chosen), dot(query[half:], chosen)])
+
+    @pl.when(inside)
+    def _():
+        for s in (0, 1):
+            arrive(behind.at[s, :, :BLOCK], 3 + s)
+
+    @pl.when(inside & (h == 1))
+    def _():
+        for s in (0, 1):
+            arrive(behind.at[s, :, BLOCK:], 5 + s)
 
     cross = None
     for s in (0, 1):
-
-        @pl.when(inside)
-        def _(s=s):
-            arrive(behind.at[s, :, :BLOCK], 3 + s)
-
-        @pl.when(inside & (h == 1))
-        def _(s=s):
-            arrive(behind.at[s, :, BLOCK:], 5 + s)
-
         edge = jnp.where(h == 0, own[s, :, :HALO], behind[s, :, BLOCK:])
         prepare(jnp.concatenate([behind[s, :, :BLOCK], edge], axis=1), 2 + s)
         for step in range(GROUP // 2):
             k = GROUP * s + 2 * step
             query = jnp.concatenate([zed[k], zed[k + 1]], axis=1)
-            product = dot(query, jnp.concatenate(normalized(2 + s, step), axis=1))
-            cross = product if cross is None else cross + product
-
+            key = jnp.concatenate(normalized(2 + s, step), axis=1)
+            cross = accumulate(cross, [dot(query, key[:half]), dot(query, key[half:])])
+
+    same = jnp.concatenate(same, axis=0)
+    cross = jnp.concatenate(cross, axis=1)
     limit = excl[0]
     apart = (
         lax.broadcasted_iota(jnp.int32, (BLOCK, half), 0)

time: 30.2 us -> 25.2 us (0.83); the launches traced: 29.6 us -> 25 us
  Pallas kernels: 27.7 us -> 23.1 us
    pallas_call x1, Pallas kernels: 27.7 us -> 23.1 us  [on_device(): pl.pallas_call(lambda *refs: kernel(blocks, *refs), out_shape=jax.ShapeDt...]
where the time goes in v3:
time: 25.2 us; the launch traced here: 25 us
  Pallas kernels  23.1 us (92%)
  local copies, waits for them, and re-layouts  1.26 us (5%)
  between operations  0.66 us (3%)
    pallas_call x1, Pallas kernels, on_device(): pl.pallas_call(lambda *refs: kernel(blocks, *refs), out_shape=jax.ShapeDt...  23.1 us
    unnamed x1, local copies, waits for them, and re-layouts  1.26 us

profile of v3, /device:TPU:199, one launch (start us, length us, event | category | flops | bytes accessed | tf_op | source)
XLA Modules:
  0.0 25.0 jit_solution(2238927089003825762)
XLA Ops:
  0.7 23.1 %shard_map.37 = f32[1,512]{1,0:T(1,128)} custom-call(f32[32,512]{1,0:T(8,128)} %refs_0_.1, f32[32,127]{1,0:T(8,128)} %refs_1_.1, s32[1]{0:T(128)S(6)} %copy.5.refs_2_), custom_call_target="tpu_custom_call" | custom-call | tf_op jit(solution)/shard_map/pallas_call | solution.py:318
  23.7 1.3 %copy.6 = f32[512]{0:T(512)} copy(f32[512]{0:T(512)} %bitcast.1) | data formatting | bytes 4096

commit v4 on v3

--- a/solution.py
+++ b/solution.py
@@ -63,7 +63,7 @@
 
 def kernel(
     blocks, series, tail, excl, out,
-    own, behind, rest, ending, lanes, center, factor, zed,
+    own, behind, rest, ending, lanes, center, factor, zed, within,
     row_out, row_in, col_out, near_in, far_in,
     local, send, recv, ready,
 ):
@@ -82,6 +82,7 @@
 
     opens_row = lax.rem(t, ROW) == 0
     closes_row = lax.rem(t, ROW) == ROW - 1
+    ends_row = lax.rem(t, ROW) >= ROW - 2
     signal(barrier, (t, 1 - h))
 
     @pl.when((after >= 1) & jnp.logical_not(closes_row))
@@ -130,24 +131,28 @@
         for chan in (0, 1):
             signal(ready, (t + 1, chan))
 
+    def send_ahead():
+        @pl.when(after >= 1)
+        def _():
+            next_block.start()
+
+        @pl.when((after >= 1) & (t >= 1))
+        def _():
+            next_edge.start()
+
+        @pl.when(after >= 2)
+        def _():
+            second_block.start()
+
+    pl.when(ends_row)(send_ahead)
+
     @pl.when(jnp.logical_not(opens_row))
     def _():
         for edge in edges:
             edge.start()
 
     share.start()
-
-    @pl.when(after >= 1)
-    def _():
-        next_block.start()
-
-    @pl.when((after >= 1) & (t >= 1))
-    def _():
-        next_edge.start()
-
-    @pl.when(after >= 2)
-    def _():
-        second_block.start()
+    pl.when(jnp.logical_not(ends_row))(send_ahead)
 
     @pl.when(opens_row & (t >= 1))
     def _():
@@ -184,6 +189,24 @@
             parts.append((shifted * factor[index]).astype(jnp.bfloat16))
         return parts
 
+    def receive(s):
+        @pl.when(inside)
+        def _():
+            arrive(behind.at[s, :, :BLOCK], 3 + s)
+
+        @pl.when(inside & (h == 1))
+        def _():
+            arrive(behind.at[s, :, BLOCK:], 5 + s)
+
+    def prepare_behind(s):
+        edge = jnp.where(h == 0, own[s, :, :HALO], behind[s, :, BLOCK:])
+        prepare(jnp.concatenate([behind[s, :, :BLOCK], edge], axis=1), 2 + s)
+
+    @pl.when(closes_row)
+    def _():
+        receive(0)
+        prepare_behind(0)
+
     half = BLOCK // 2
     same = None
 
@@ -191,10 +214,12 @@
     def _():
         arrive(own.at[0, :, BLOCK:], 1)
 
+    prepare(own[0], 0)
     arrive(own.at[1, :, BLOCK:], 2)
     arrive(own.at[1, :, :BLOCK], 0)
     for s in (0, 1):
-        prepare(own[s], s)
+        if s == 1:
+            prepare(own[1], 1)
         for step in range(GROUP // 2):
             parts = normalized(s, step)
             for j in (0, 1):
@@ -203,35 +228,33 @@
             chosen = jnp.where(h == 0, query[:half], query[half:])
             same = accumulate(same, [dot(query[:half], chosen), dot(query[half:], chosen)])
 
-    @pl.when(inside)
-    def _():
-        for s in (0, 1):
-            arrive(behind.at[s, :, :BLOCK], 3 + s)
-
-    @pl.when(inside & (h == 1))
-    def _():
-        for s in (0, 1):
-            arrive(behind.at[s, :, BLOCK:], 5 + s)
-
-    cross = None
-    for s in (0, 1):
-        edge = jnp.where(h == 0, own[s, :, :HALO], behind[s, :, BLOCK:])
-        prepare(jnp.concatenate([behind[s, :, :BLOCK], edge], axis=1), 2 + s)
-        for step in range(GROUP // 2):
-            k = GROUP * s + 2 * step
-            query = jnp.concatenate([zed[k], zed[k + 1]], axis=1)
-            key = jnp.concatenate(normalized(2 + s, step), axis=1)
-            cross = accumulate(cross, [dot(query, key[:half]), dot(query, key[half:])])
-
+    limit = excl[0]
     same = jnp.concatenate(same, axis=0)
-    cross = jnp.concatenate(cross, axis=1)
-    limit = excl[0]
     apart = (
         lax.broadcasted_iota(jnp.int32, (BLOCK, half), 0)
         - lax.broadcasted_iota(jnp.int32, (BLOCK, half), 1)
         - half * h
     )
     same = jnp.where(jnp.abs(apart) >= limit, same, MASKED)
+    within[...] = jnp.maximum(same[:, :HALO], same[:, HALO:])
+
+    @pl.when(jnp.logical_not(closes_row))
+    def _():
+        receive(0)
+        prepare_behind(0)
+
+    receive(1)
+    cross = None
+    for s in (0, 1):
+        if s == 1:
+            prepare_behind(1)
+        for step in range(GROUP // 2):
+            k = GROUP * s + 2 * step
+            query = jnp.concatenate([zed[k], zed[k + 1]], axis=1)
+            key = jnp.concatenate(normalized(2 + s, step), axis=1)
+            cross = accumulate(cross, [dot(query, key[:half]), dot(query, key[half:])])
+
+    cross = jnp.concatenate(cross, axis=1)
 
     reach = (
         lax.broadcasted_iota(jnp.int32, (HALO, HALO), 0)
@@ -262,7 +285,7 @@
     for tile in tiles[1:]:
         best = jnp.maximum(best, tile)
     best = jnp.where(inside, best, MASKED)
-    best = jnp.maximum(best, jnp.maximum(same[:, :HALO], same[:, HALO:]))
+    best = jnp.maximum(best, within[...])
     rows = jnp.max(best.T, axis=0, keepdims=True)
     row_out[...] = rows
 
@@ -317,7 +340,7 @@
         f32 = jnp.float32
         result = pl.pallas_call(
             lambda *refs: kernel(blocks, *refs),
-            out_shape=jax.ShapeDtypeStruct((1, BLOCK), f32),
+            out_shape=pltpu.VMEM((1, BLOCK), f32),
             in_specs=[hbm, hbm, pl.BlockSpec(memory_space=pltpu.SMEM)],
             out_specs=vmem,
             scratch_shapes=[
@@ -329,6 +352,7 @@
                 pltpu.VMEM((4, BLOCK, M), f32),
                 pltpu.VMEM((4, BLOCK, M), f32),
                 pltpu.VMEM((2 * GROUP, BLOCK, M), jnp.bfloat16),
+                pltpu.VMEM((BLOCK, HALO), f32),
             ]
             + [pltpu.VMEM((1, BLOCK), f32)] * 5
             + [
@@ -338,7 +362,7 @@
                 pltpu.SemaphoreType.REGULAR,
             ],
             compiler_params=pltpu.CompilerParams(
-                collective_id=0, has_side_effects=True, vmem_limit_bytes=64 * 1024 * 1024
+                collective_id=0, has_side_effects=True, vmem_limit_bytes=60 * 1024 * 1024
             ),
         )(series, tail, excl)
         return result.reshape(BLOCK)

time: 25.2 us -> 23.7 us (0.940); the launches traced: 25 us -> 23.2 us
  Pallas kernels: 23.1 us -> 22 us
  local copies, waits for them, and re-layouts: 1.26 us -> 0.58 us
    pallas_call x1, Pallas kernels: 23.1 us -> 22 us  [on_device(): pl.pallas_call(lambda *refs: kernel(blocks, *refs), out_shape=pltpu.VMEM(...]
    unnamed x1, local copies, waits for them, and re-layouts: 1.26 us -> 0.58 us
where the time goes in v4:
time: 23.7 us; the launch traced here: 23.2 us
  Pallas kernels  22 us (93%)
  between operations  0.66 us (3%)
  local copies, waits for them, and re-layouts  0.58 us (2%)
    pallas_call x1, Pallas kernels, on_device(): pl.pallas_call(lambda *refs: kernel(blocks, *refs), out_shape=pltpu.VMEM(...  22 us
    unnamed x1, local copies, waits for them, and re-layouts  0.58 us

profile of v4, /device:TPU:199, one launch (start us, length us, event | category | flops | bytes accessed | tf_op | source)
XLA Modules:
  0.0 23.2 jit_solution(5172884694826197143)
XLA Ops:
  0.7 22.0 %shard_map.37 = f32[1,512]{1,0:T(1,128)S(1)} custom-call(f32[32,512]{1,0:T(8,128)} %refs_0_.1, f32[32,127]{1,0:T(8,128)} %refs_1_.1, s32[1]{0:T(128)S(6)} %copy.6.refs_2_), custom_call_target="tpu_custom_call" | custom-call | tf_op jit(solution)/shard_map/pallas_call | solution.py:341
  22.6 0.6 %copy.5 = f32[512]{0:T(512)} copy(f32[512]{0:T(512)S(1)} %bitcast.1) | data formatting | bytes 4096

commit v5 on v4

--- a/solution.py
+++ b/solution.py
@@ -214,12 +214,11 @@
     def _():
         arrive(own.at[0, :, BLOCK:], 1)
 
-    prepare(own[0], 0)
-    arrive(own.at[1, :, BLOCK:], 2)
-    arrive(own.at[1, :, :BLOCK], 0)
     for s in (0, 1):
         if s == 1:
-            prepare(own[1], 1)
+            arrive(own.at[1, :, BLOCK:], 2)
+            arrive(own.at[1, :, :BLOCK], 0)
+        prepare(own[s], s)
         for step in range(GROUP // 2):
             parts = normalized(s, step)
             for j in (0, 1):

time: 23.7 us -> 23.7 us (level); the launches traced: 23.2 us -> 23.5 us
  Pallas kernels: 22 us -> 22.3 us
    pallas_call x1, Pallas kernels: 22 us -> 22.3 us  [on_device(): pl.pallas_call(lambda *refs: kernel(blocks, *refs), out_shape=pltpu.VMEM(...]
where the time goes in v5:
time: 23.7 us; the launch traced here: 23.5 us
  Pallas kernels  22.3 us (94%)
  between operations  0.66 us (3%)
  local copies, waits for them, and re-layouts  0.58 us (2%)
    pallas_call x1, Pallas kernels, on_device(): pl.pallas_call(lambda *refs: kernel(blocks, *refs), out_shape=pltpu.VMEM(...  22.3 us
    unnamed x1, local copies, waits for them, and re-layouts  0.58 us

profile of v5, /device:TPU:199, one launch (start us, length us, event | category | flops | bytes accessed | tf_op | source)
XLA Modules:
  0.0 23.5 jit_solution(6353994762684194691)
XLA Ops:
  0.7 22.3 %shard_map.37 = f32[1,512]{1,0:T(1,128)S(1)} custom-call(f32[32,512]{1,0:T(8,128)} %refs_0_.1, f32[32,127]{1,0:T(8,128)} %refs_1_.1, s32[1]{0:T(128)S(6)} %copy.6.refs_2_), custom_call_target="tpu_custom_call" | custom-call | tf_op jit(solution)/shard_map/pallas_call | solution.py:340
  22.9 0.6 %copy.5 = f32[512]{0:T(512)} copy(f32[512]{0:T(512)S(1)} %bitcast.1) | data formatting | bytes 4096
